TPU v7x, 32 devices: a whole 2x2x4 slice. The times are simulated.
32 devices in a mesh: grp: 8 (over z, x), rep: 4 (over y, core).
Axes of the slice: x: 2, y: 2, z: 4, core: 2. Of those that a mesh axis runs over, the one named last changes fastest.
Arguments:
- series: bfloat16 [256, 5632], P('grp'), may hold values from -6 to 6
- regressors: float32 [256, 24], P('grp'), may hold values from -3 to 3
- span_ids: int32 [256], replicated, may hold values from 0 to 3, never falling along the last dimension, each value on 1 to 128 neighbouring positions
- nuisance_count: int32 [1], replicated, may hold values from 12 to 24
- owner_order: int32 [8], replicated, may hold values from 0 to 7
- vectors: bfloat16 [5632, 64], P('grp'), may hold values from -0.3125 to 0.3125
Outputs:
- projected: float32 [5632, 64], P(('grp', 'rep'))
Inputs may be any that keep to these rules, and one draw needn't show every extreme that they name: `span_ids`: never falls along frames; each of the 4 spans holds 1 to 128 frames, one exactly 128. `owner_order`: blocks may name the same slab.
All inputs are finite; a program needn't handle non-finite values.
Results may differ from a plain program's by a relative error of at most 0.0095.
Values may be sent and summed in bfloat16 or wider, within the bound.
A program may use at most 64 MiB of HBM per device.

v0:
```python
import math
import jax
import jax.numpy as jnp
from jax import lax
from jax.sharding import PartitionSpec as P

BLOCKS = 8
fast_pole = 0.64
slow_pole = 0.955
corr_limit = 0.99
norm_eps = 1e-06


def spread_2(value, axis, root):
    mine = lax.axis_index(axis) == root
    return lax.psum(jnp.where(mine, value, jnp.zeros_like(value)), axis)


def fisher_map(correlation):
    clipped = jnp.clip(correlation, -corr_limit, corr_limit)
    return 0.5 * jnp.log((1.0 + clipped) / (1.0 - clipped))


def block_operators(span_ids, frames):
    offsets = jnp.arange(128)
    lag_steps = offsets[:, None] - offsets[None, :]
    lag_clip = jnp.maximum(lag_steps, 0).astype(jnp.float32)
    operators = []
    for number in range(frames // 128):
        ids_here = span_ids[number * 128 : (number + 1) * 128]
        joined = (ids_here[:, None] == ids_here[None, :]) & (lag_steps >= 0)
        if number == 0:
            linked = jnp.zeros((128,), jnp.float32)
        else:
            linked = (ids_here == span_ids[number * 128 - 1]).astype(jnp.float32)
        pole_pair = []
        for pole_value in (fast_pole, slow_pole):
            matrix = jnp.where(
                joined, (1.0 - pole_value) * jnp.exp(lag_clip * math.log(pole_value)), 0.0
            )
            carried = linked * jnp.exp((offsets + 1).astype(jnp.float32) * math.log(pole_value))
            pole_pair.append((matrix, carried))
        operators.append(pole_pair)
    return operators


def band_pass(columns_in, operators):
    col_count = columns_in.shape[1]
    states = [jnp.zeros((col_count,), jnp.float32), jnp.zeros((col_count,), jnp.float32)]
    pieces = []
    for number, pole_pair in enumerate(operators):
        segment = columns_in[number * 128 : (number + 1) * 128]
        outputs = []
        for pole_slot in range(2):
            matrix, carried = pole_pair[pole_slot]
            response = (
                jnp.dot(matrix, segment, precision=lax.Precision.HIGHEST)
                + carried[:, None] * states[pole_slot][None, :]
            )
            states[pole_slot] = response[-1]
            outputs.append(response)
        pieces.append(outputs[0] - outputs[1])
    return jnp.concatenate(pieces, axis=0)


def nuisance_basis(filtered_nuisance, nuisance_count):
    active = (jnp.arange(filtered_nuisance.shape[1]) < nuisance_count[0]).astype(jnp.float32)
    masked = filtered_nuisance * active[None, :]
    gram_matrix = jnp.dot(masked.T, masked, precision=lax.Precision.HIGHEST) + jnp.diag(
        1.0 - active
    )
    return (masked, jnp.linalg.cholesky(gram_matrix))


def scale_columns(filtered, masked, lower_factor):
    highest = lax.Precision.HIGHEST
    right_side = jnp.dot(masked.T, filtered, precision=highest)
    halfway = lax.linalg.triangular_solve(lower_factor, right_side, left_side=True, lower=True)
    coefficients = lax.linalg.triangular_solve(
        lower_factor, halfway, left_side=True, lower=True, transpose_a=True
    )
    cleaned = filtered - jnp.dot(masked, coefficients, precision=highest)
    centered = cleaned - jnp.mean(cleaned, axis=0, keepdims=True)
    spread = lax.rsqrt(jnp.mean(centered * centered, axis=0, keepdims=True) + norm_eps)
    return (centered * spread * (1.0 / math.sqrt(centered.shape[0]))).astype(jnp.bfloat16)


def fold_tile(my_cols, vec_slab, running, part_cols):
    correlation = lax.dot_general(
        my_cols, part_cols, (((0,), (0,)), ((), ())), preferred_element_type=jnp.float32
    )
    fisher = fisher_map(correlation).astype(jnp.bfloat16)
    return running + jnp.dot(fisher, vec_slab, preferred_element_type=jnp.float32)


def local(series, regressors, span_ids, nuisance_count, owner_order, vectors):
    grp_count = lax.axis_size("grp")
    rep_count = lax.axis_size("rep")
    rep_index = lax.axis_index("rep")
    frames_loc = series.shape[0]
    frames = frames_loc * grp_count
    own_cols = series.shape[1] // (grp_count * rep_count)
    operators = block_operators(span_ids, frames)
    nuisance = lax.all_gather(regressors, "grp", axis=0, tiled=True)
    masked, lower_factor = nuisance_basis(band_pass(nuisance, operators), nuisance_count)
    quarter = series.reshape(frames_loc, grp_count, rep_count, own_cols)
    quarter = lax.dynamic_slice_in_dim(quarter, rep_index, 1, 2).reshape(
        frames_loc, grp_count, own_cols
    )
    filtered = band_pass(
        lax.all_to_all(quarter, "grp", split_axis=1, concat_axis=0, tiled=True)[:, 0, :].astype(
            jnp.float32
        ),
        operators,
    )
    unit_cols = scale_columns(filtered, masked, lower_factor)
    projected = jnp.zeros((own_cols, vectors.shape[1]), jnp.float32)
    for number in range(BLOCKS):
        piece_in, vec_slab = (
            spread_2(unit_cols, "grp", owner_order[number]),
            spread_2(vectors, "grp", owner_order[number]),
        )
        projected = fold_tile(
            unit_cols, vec_slab, projected, lax.all_gather(piece_in, "rep", axis=1, tiled=True)
        )
    return projected


def solution(mesh):
    placed = (P("grp", None), P("grp", None), P(), P(), P(), P("grp", None))
    return jax.shard_map(
        local, mesh=mesh, in_specs=placed, out_specs=P(("grp", "rep"), None), check_vma=False
    )
```

profile of v0, /device:TPU:0, one launch (start us, length us, event | category | flops | bytes accessed | tf_op | source)
XLA Modules:
  0.0 231.1 jit_solution(4362847719951692597)
XLA Ops:
  6.5 2.0 reshape.62
  8.8 0.7 copy.24
  9.6 7.3 %all-to-all-start = ((bf16[32,8,176]{2,0,1:T(8,128)(2,1)}), bf16[32,8,176]{2,0,1:T(8,128)(2,1)S(1)}, u32[]{:S(2)}, u32[]{:S(2)}) async-start(bf16[32,8,176]{2,0,1:T(8,128)(2,1)} %bitcast.70), calls=%async_computation | async-start | bytes 262144 | tf_op jit(solution)/shard_map/all_to_all | solution.py:111
  16.9 0.7 copy-done.10
  18.8 0.7 compare_select_fusion
  19.5 0.7 fusion.173
  25.2 31.1 %all-gather = f32[8,32,24]{1,2,0:T(8,128)S(1)} all-gather(f32[1,32,24]{1,2,0:T(8,128)S(1)} %bitcast.78), channel_id=1, replica_groups=mesh['grp'=8,'rep'=4] {'grp'}, dimensions={0}, use_global_device_ids=true | all-gather | bytes 27648 | tf_op jit(solution)/shard_map/all_gather | solution.py:104
  58.4 2.2 cholesky.16
  60.7 0.6 compare_reduce_fusion
  61.3 0.6 fusion.93
  62.0 1.9 custom-call.8
  63.8 0.9 broadcast_select_fusion
  67.6 0.8 broadcast_select_fusion.8
  68.4 0.9 broadcast_select_fusion.9
  69.3 95.1 %all-reduce.3.cloned.1.call-done = (bf16[704,64]{0,1:T(8,128)(2,1)}, bf16[256,176]{0,1:T(8,128)(2,1)}, bf16[704,64]{0,1:T(8,128)(2,1)}, bf16[256,176]{0,1:T(8,12...) async-done(((bf16[704,64]{0,1:T(8,128)(2,1)}, ...) | async-done | bytes 1441808 | tf_op jit(solution)/shard_map/psum | solution.py:16
  164.5 6.7 %all_gather.28 = bf16[256,704]{0,1:T(8,128)(2,1)S(1)} all-gather(bf16[256,176]{0,1:T(8,128)(2,1)} %get-tuple-element.6), channel_id=1, replica_groups=mesh['grp'=8,'rep'=4] {'rep'}, dimensions={1}, use_global_device_ids=true | all-gather | bytes 450560 | tf_op jit(solution)/shard_map/all_gather | solution.py:124
  171.2 6.5 %all_gather.29 = bf16[256,704]{0,1:T(8,128)(2,1)S(1)} all-gather(bf16[256,176]{0,1:T(8,128)(2,1)S(1)} %copy-done.7), channel_id=1, replica_groups=mesh['grp'=8,'rep'=4] {'rep'}, dimensions={1}, use_global_device_ids=true | all-gather | bytes 450560 | tf_op jit(solution)/shard_map/all_gather | solution.py:124
  177.7 6.5 %all_gather.30 = bf16[256,704]{0,1:T(8,128)(2,1)S(1)} all-gather(bf16[256,176]{0,1:T(8,128)(2,1)S(1)} %copy-done.6), channel_id=1, replica_groups=mesh['grp'=8,'rep'=4] {'rep'}, dimensions={1}, use_global_device_ids=true | all-gather | bytes 450560 | tf_op jit(solution)/shard_map/all_gather | solution.py:124
  184.2 6.5 %all_gather.31 = bf16[256,704]{0,1:T(8,128)(2,1)S(1)} all-gather(bf16[256,176]{0,1:T(8,128)(2,1)S(1)} %copy-done.5), channel_id=1, replica_groups=mesh['grp'=8,'rep'=4] {'rep'}, dimensions={1}, use_global_device_ids=true | all-gather | bytes 450560 | tf_op jit(solution)/shard_map/all_gather | solution.py:124
  190.7 6.5 %all_gather.32 = bf16[256,704]{0,1:T(8,128)(2,1)S(1)} all-gather(bf16[256,176]{0,1:T(8,128)(2,1)S(1)} %copy-done.4), channel_id=1, replica_groups=mesh['grp'=8,'rep'=4] {'rep'}, dimensions={1}, use_global_device_ids=true | all-gather | bytes 450560 | tf_op jit(solution)/shard_map/all_gather | solution.py:124
  197.3 6.5 %all_gather.33 = bf16[256,704]{0,1:T(8,128)(2,1)S(1)} all-gather(bf16[256,176]{0,1:T(8,128)(2,1)S(1)} %copy-done.3), channel_id=1, replica_groups=mesh['grp'=8,'rep'=4] {'rep'}, dimensions={1}, use_global_device_ids=true | all-gather | bytes 450560 | tf_op jit(solution)/shard_map/all_gather | solution.py:124
  203.8 6.5 %all_gather.34 = bf16[256,704]{0,1:T(8,128)(2,1)S(1)} all-gather(bf16[256,176]{0,1:T(8,128)(2,1)S(1)} %copy-done.2), channel_id=1, replica_groups=mesh['grp'=8,'rep'=4] {'rep'}, dimensions={1}, use_global_device_ids=true | all-gather | bytes 450560 | tf_op jit(solution)/shard_map/all_gather | solution.py:124
  210.3 6.5 %all_gather.35 = bf16[256,704]{0,1:T(8,128)(2,1)S(1)} all-gather(bf16[256,176]{0,1:T(8,128)(2,1)S(1)} %copy-done.1), channel_id=1, replica_groups=mesh['grp'=8,'rep'=4] {'rep'}, dimensions={1}, use_global_device_ids=true | all-gather | bytes 450560 | tf_op jit(solution)/shard_map/all_gather | solution.py:124
  223.1 1.1 convolution_add_fusion.4
  (83 shorter events, 12.1 us)
Async XLA Ops:
  9.6 55.2 %all-to-all-start = ((bf16[32,8,176]{2,0,1:T(8,128)(2,1)}), bf16[32,8,176]{2,0,1:T(8,128)(2,1)S(1)}, u32[]{:S(2)}, u32[]{:S(2)}) async-start(bf16[32,8,176]{2,0,1:T(8,128)(2,1)} %bitcast.70), calls=%async_computation | async-start | bytes 262144 | tf_op jit(solution)/shard_map/all_to_all | solution.py:111
  16.8 147.6 %all-reduce.3.cloned.1.call-start = ((), (), s32[]{:S(2)}) async-start(), calls=%async_computation.1 | async-start | bytes 3014656 | tf_op jit(solution)/shard_map/psum | solution.py:16
  16.9 0.7 copy-start.10
  18.8 0.7 copy-start.8
  22.6 2.6 %copy-start.9 = (f32[32,24]{0,1:T(8,128)S(1)}, f32[32,24]{0,1:T(8,128)}, u32[]{:S(2)}) copy-start(f32[32,24]{0,1:T(8,128)} %param.7) | copy-start | bytes 9220
  58.1 5.8 %copy-start = (bf16[704,64]{0,1:T(8,128)(2,1)S(1)}, bf16[704,64]{0,1:T(8,128)(2,1)}, u32[]{:S(2)}) copy-start(bf16[704,64]{0,1:T(8,128)(2,1)} %param.11) | copy-start | bytes 270340
  164.5 6.7 %copy-start.7 = (bf16[256,176]{0,1:T(8,128)(2,1)S(1)}, bf16[256,176]{0,1:T(8,128)(2,1)}, u32[]{:S(2)}) copy-start(bf16[256,176]{0,1:T(8,128)(2,1)} %get-tuple-element.8) | copy-start | bytes 270340
  171.2 6.5 %copy-start.6 = (bf16[256,176]{0,1:T(8,128)(2,1)S(1)}, bf16[256,176]{0,1:T(8,128)(2,1)}, u32[]{:S(2)}) copy-start(bf16[256,176]{0,1:T(8,128)(2,1)} %get-tuple-element.10) | copy-start | bytes 270340
  177.7 6.5 %copy-start.5 = (bf16[256,176]{0,1:T(8,128)(2,1)S(1)}, bf16[256,176]{0,1:T(8,128)(2,1)}, u32[]{:S(2)}) copy-start(bf16[256,176]{0,1:T(8,128)(2,1)} %get-tuple-element.12) | copy-start | bytes 270340
  184.2 6.5 %copy-start.4 = (bf16[256,176]{0,1:T(8,128)(2,1)S(1)}, bf16[256,176]{0,1:T(8,128)(2,1)}, u32[]{:S(2)}) copy-start(bf16[256,176]{0,1:T(8,128)(2,1)} %get-tuple-element.14) | copy-start | bytes 270340
  190.7 6.5 %copy-start.3 = (bf16[256,176]{0,1:T(8,128)(2,1)S(1)}, bf16[256,176]{0,1:T(8,128)(2,1)}, u32[]{:S(2)}) copy-start(bf16[256,176]{0,1:T(8,128)(2,1)} %get-tuple-element.16) | copy-start | bytes 270340
  197.3 6.5 %copy-start.2 = (bf16[256,176]{0,1:T(8,128)(2,1)S(1)}, bf16[256,176]{0,1:T(8,128)(2,1)}, u32[]{:S(2)}) copy-start(bf16[256,176]{0,1:T(8,128)(2,1)} %get-tuple-element.18) | copy-start | bytes 270340
  203.8 6.5 %copy-start.1 = (bf16[256,176]{0,1:T(8,128)(2,1)S(1)}, bf16[256,176]{0,1:T(8,128)(2,1)}, u32[]{:S(2)}) copy-start(bf16[256,176]{0,1:T(8,128)(2,1)} %get-tuple-element.20) | copy-start | bytes 270340
  210.3 6.5 %copy-start.18 = (bf16[704,64]{0,1:T(8,128)(2,1)S(1)}, bf16[704,64]{0,1:T(8,128)(2,1)}, u32[]{:S(2)}) copy-start(bf16[704,64]{0,1:T(8,128)(2,1)} %get-tuple-element.5) | copy-start | bytes 270340
  216.8 0.9 copy-start.17
  217.7 0.9 copy-start.16
  218.6 0.9 copy-start.15
  219.5 0.9 copy-start.14
  220.4 0.9 copy-start.13
  221.3 0.9 copy-start.12
  222.2 0.9 copy-start.11
Sparse Core Ops, SparseCore 0:
  69.4 94.9 all-reduce.2
where the time goes:
time: 232 us; the launch traced here: 231 us
  waiting for transfers between devices  95.1 us (41%)
  blocking collectives  83.4 us (36%)
  between operations  19.4 us (8%)
  other arithmetic  8.9 us (4%)
  local copies, waits for them, and re-layouts  8.67 us (4%)
  matrix products  8.23 us (4%)
  starting transfers between devices  7.29 us (3%)
    psum x1, waiting for transfers between devices, spread_2(): return lax.psum(jnp.where(mine, value, jnp.zeros_like(value)), axis)  95.1 us
    all_gather x8, blocking collectives, local(): lax.all_gather(piece_in, 'rep', axis=1, tiled=True)  52.3 us
    all_gather x1, blocking collectives, local(): nuisance = lax.all_gather(regressors, 'grp', axis=0, tiled=True)  31.1 us
    all_to_all x1, starting transfers between devices, local(): lax.all_to_all(quarter, 'grp', split_axis=1, concat_axis=0, tiled=True)  7.25 us
    dot_general x8, matrix products, fold_tile(): jnp.dot(fisher, vec_slab, preferred_element_type=jnp.float32)  4.66 us
  transfers between devices with their start and end apart: 2, of which 1 were waited for; matrix products, arithmetic and copies ran while one was open for 4% of the time, Pallas kernels for 0%

commit v1 on v0

--- a/solution.py
+++ b/solution.py
@@ -108,9 +108,12 @@
         frames_loc, grp_count, own_cols
     )
     filtered = band_pass(
-        lax.all_to_all(quarter, "grp", split_axis=1, concat_axis=0, tiled=True)[:, 0, :].astype(
-            jnp.float32
-        ),
+        jnp.concatenate(
+            lax.all_to_all(
+                jnp.stack(jnp.split(quarter, lax.axis_size("grp"), axis=1)), "grp", 0, 0
+            ),
+            axis=0,
+        )[:, 0, :].astype(jnp.float32),
         operators,
     )
     unit_cols = scale_columns(filtered, masked, lower_factor)

time: 232 us -> 236 us (1.017)
  local copies, waits for them, and re-layouts: 8.67 us -> 13 us
    unnamed x38 -> x46, local copies, waits for them, and re-layouts: 3.38 us -> 7.62 us
where the time goes in v1:
time: 236 us
  waiting for transfers between devices  95.1 us (40%)
  blocking collectives  83.4 us (35%)
  between operations  19.5 us (8%)
  local copies, waits for them, and re-layouts  13 us (6%)
  other arithmetic  8.86 us (4%)
  matrix products  8.23 us (3%)
  starting transfers between devices  7.29 us (3%)
    psum x1, waiting for transfers between devices, spread_2(): return lax.psum(jnp.where(mine, value, jnp.zeros_like(value)), axis)  95.1 us
    all_gather x8, blocking collectives, local(): lax.all_gather(piece_in, 'rep', axis=1, tiled=True)  52.3 us
    all_gather x1, blocking collectives, local(): nuisance = lax.all_gather(regressors, 'grp', axis=0, tiled=True)  31.1 us
    unnamed x46, local copies, waits for them, and re-layouts  7.62 us
    all_to_all x1, starting transfers between devices, local(): lax.all_to_all(jnp.stack(jnp.split(quarter, lax.axis_size('grp'), axis=1)...  7.25 us
  transfers between devices with their start and end apart: 2, of which 1 were waited for; matrix products, arithmetic and copies ran while one was open for 4% of the time, Pallas kernels for 0%

profile of v1, /device:TPU:0, one launch (start us, length us, event | category | flops | bytes accessed | tf_op | source)
XLA Modules:
  0.0 235.5 jit_solution(630950272272020619)
XLA Ops:
  6.5 2.0 reshape.61
  10.3 0.6 constant_dynamic-update-slice_fusion.5
  13.9 7.3 %all-to-all-start = ((bf16[8,32,1,176]{3,1,2,0:T(8,128)(2,1)}), bf16[8,32,1,176]{3,1,2,0:T(8,128)(2,1)S(1)}, u32[]{:S(2)}, u32[]{:S(2)}) async-start(bf16[8,32,1,176]{3,1,2,0:T(8,128)(2,1)} %constant_dynamic-update-slice_fusion), calls=%async_computation | async-start | bytes 262144 | tf_op jit(solution)/shard_map/all_to_all | solution.py:112
  21.3 0.7 copy-done.10
  23.2 0.7 compare_select_fusion
  23.9 0.7 fusion.174
  29.7 31.1 %all-gather = f32[8,32,24]{1,2,0:T(8,128)S(1)} all-gather(f32[1,32,24]{1,2,0:T(8,128)S(1)} %bitcast.91), channel_id=1, replica_groups=mesh['grp'=8,'rep'=4] {'grp'}, dimensions={0}, use_global_device_ids=true | all-gather | bytes 27648 | tf_op jit(solution)/shard_map/all_gather | solution.py:104
  62.9 2.2 cholesky.16
  65.2 0.6 compare_reduce_fusion
  65.8 0.6 fusion.93
  66.5 1.9 custom-call.8
  68.3 0.9 broadcast_select_fusion
  72.1 0.8 broadcast_select_fusion.8
  72.9 0.9 broadcast_select_fusion.9
  73.8 95.1 %all-reduce.3.cloned.1.call-done = (bf16[704,64]{0,1:T(8,128)(2,1)}, bf16[256,176]{0,1:T(8,128)(2,1)}, bf16[704,64]{0,1:T(8,128)(2,1)}, bf16[256,176]{0,1:T(8,12...) async-done(((bf16[704,64]{0,1:T(8,128)(2,1)}, ...) | async-done | bytes 1441808 | tf_op jit(solution)/shard_map/psum | solution.py:16
  168.9 6.7 %all_gather.28 = bf16[256,704]{0,1:T(8,128)(2,1)S(1)} all-gather(bf16[256,176]{0,1:T(8,128)(2,1)} %get-tuple-element.6), channel_id=1, replica_groups=mesh['grp'=8,'rep'=4] {'rep'}, dimensions={1}, use_global_device_ids=true | all-gather | bytes 450560 | tf_op jit(solution)/shard_map/all_gather | solution.py:127
  175.6 6.5 %all_gather.29 = bf16[256,704]{0,1:T(8,128)(2,1)S(1)} all-gather(bf16[256,176]{0,1:T(8,128)(2,1)S(1)} %copy-done.7), channel_id=1, replica_groups=mesh['grp'=8,'rep'=4] {'rep'}, dimensions={1}, use_global_device_ids=true | all-gather | bytes 450560 | tf_op jit(solution)/shard_map/all_gather | solution.py:127
  182.1 6.5 %all_gather.30 = bf16[256,704]{0,1:T(8,128)(2,1)S(1)} all-gather(bf16[256,176]{0,1:T(8,128)(2,1)S(1)} %copy-done.6), channel_id=1, replica_groups=mesh['grp'=8,'rep'=4] {'rep'}, dimensions={1}, use_global_device_ids=true | all-gather | bytes 450560 | tf_op jit(solution)/shard_map/all_gather | solution.py:127
  188.7 6.5 %all_gather.31 = bf16[256,704]{0,1:T(8,128)(2,1)S(1)} all-gather(bf16[256,176]{0,1:T(8,128)(2,1)S(1)} %copy-done.5), channel_id=1, replica_groups=mesh['grp'=8,'rep'=4] {'rep'}, dimensions={1}, use_global_device_ids=true | all-gather | bytes 450560 | tf_op jit(solution)/shard_map/all_gather | solution.py:127
  195.2 6.5 %all_gather.32 = bf16[256,704]{0,1:T(8,128)(2,1)S(1)} all-gather(bf16[256,176]{0,1:T(8,128)(2,1)S(1)} %copy-done.4), channel_id=1, replica_groups=mesh['grp'=8,'rep'=4] {'rep'}, dimensions={1}, use_global_device_ids=true | all-gather | bytes 450560 | tf_op jit(solution)/shard_map/all_gather | solution.py:127
  201.7 6.5 %all_gather.33 = bf16[256,704]{0,1:T(8,128)(2,1)S(1)} all-gather(bf16[256,176]{0,1:T(8,128)(2,1)S(1)} %copy-done.3), channel_id=1, replica_groups=mesh['grp'=8,'rep'=4] {'rep'}, dimensions={1}, use_global_device_ids=true | all-gather | bytes 450560 | tf_op jit(solution)/shard_map/all_gather | solution.py:127
  208.2 6.5 %all_gather.34 = bf16[256,704]{0,1:T(8,128)(2,1)S(1)} all-gather(bf16[256,176]{0,1:T(8,128)(2,1)S(1)} %copy-done.2), channel_id=1, replica_groups=mesh['grp'=8,'rep'=4] {'rep'}, dimensions={1}, use_global_device_ids=true | all-gather | bytes 450560 | tf_op jit(solution)/shard_map/all_gather | solution.py:127
  214.7 6.5 %all_gather.35 = bf16[256,704]{0,1:T(8,128)(2,1)S(1)} all-gather(bf16[256,176]{0,1:T(8,128)(2,1)S(1)} %copy-done.1), channel_id=1, replica_groups=mesh['grp'=8,'rep'=4] {'rep'}, dimensions={1}, use_global_device_ids=true | all-gather | bytes 450560 | tf_op jit(solution)/shard_map/all_gather | solution.py:127
  227.5 1.1 convolution_add_fusion.4
  (92 shorter events, 16.6 us)
Async XLA Ops:
  13.9 55.3 %all-to-all-start = ((bf16[8,32,1,176]{3,1,2,0:T(8,128)(2,1)}), bf16[8,32,1,176]{3,1,2,0:T(8,128)(2,1)S(1)}, u32[]{:S(2)}, u32[]{:S(2)}) async-start(bf16[8,32,1,176]{3,1,2,0:T(8,128)(2,1)} %constant_dynamic-update-slice_fusion), calls=%async_computation | async-start | bytes 262144 | tf_op jit(solution)/shard_map/all_to_all | solution.py:112
  21.2 147.7 %all-reduce.3.cloned.1.call-start = ((), (), s32[]{:S(2)}) async-start(), calls=%async_computation.1 | async-start | bytes 3014656 | tf_op jit(solution)/shard_map/psum | solution.py:16
  21.2 0.7 copy-start.10
  23.2 0.7 copy-start.8
  27.1 2.6 %copy-start.9 = (f32[32,24]{0,1:T(8,128)S(1)}, f32[32,24]{0,1:T(8,128)}, u32[]{:S(2)}) copy-start(f32[32,24]{0,1:T(8,128)} %param.7) | copy-start | bytes 9220
  62.5 5.8 %copy-start = (bf16[704,64]{0,1:T(8,128)(2,1)S(1)}, bf16[704,64]{0,1:T(8,128)(2,1)}, u32[]{:S(2)}) copy-start(bf16[704,64]{0,1:T(8,128)(2,1)} %param.11) | copy-start | bytes 270340
  168.9 6.7 %copy-start.7 = (bf16[256,176]{0,1:T(8,128)(2,1)S(1)}, bf16[256,176]{0,1:T(8,128)(2,1)}, u32[]{:S(2)}) copy-start(bf16[256,176]{0,1:T(8,128)(2,1)} %get-tuple-element.8) | copy-start | bytes 270340
  175.6 6.5 %copy-start.6 = (bf16[256,176]{0,1:T(8,128)(2,1)S(1)}, bf16[256,176]{0,1:T(8,128)(2,1)}, u32[]{:S(2)}) copy-start(bf16[256,176]{0,1:T(8,128)(2,1)} %get-tuple-element.10) | copy-start | bytes 270340
  182.1 6.5 %copy-start.5 = (bf16[256,176]{0,1:T(8,128)(2,1)S(1)}, bf16[256,176]{0,1:T(8,128)(2,1)}, u32[]{:S(2)}) copy-start(bf16[256,176]{0,1:T(8,128)(2,1)} %get-tuple-element.12) | copy-start | bytes 270340
  188.7 6.5 %copy-start.4 = (bf16[256,176]{0,1:T(8,128)(2,1)S(1)}, bf16[256,176]{0,1:T(8,128)(2,1)}, u32[]{:S(2)}) copy-start(bf16[256,176]{0,1:T(8,128)(2,1)} %get-tuple-element.14) | copy-start | bytes 270340
  195.2 6.5 %copy-start.3 = (bf16[256,176]{0,1:T(8,128)(2,1)S(1)}, bf16[256,176]{0,1:T(8,128)(2,1)}, u32[]{:S(2)}) copy-start(bf16[256,176]{0,1:T(8,128)(2,1)} %get-tuple-element.16) | copy-start | bytes 270340
  201.7 6.5 %copy-start.2 = (bf16[256,176]{0,1:T(8,128)(2,1)S(1)}, bf16[256,176]{0,1:T(8,128)(2,1)}, u32[]{:S(2)}) copy-start(bf16[256,176]{0,1:T(8,128)(2,1)} %get-tuple-element.18) | copy-start | bytes 270340
  208.2 6.5 %copy-start.1 = (bf16[256,176]{0,1:T(8,128)(2,1)S(1)}, bf16[256,176]{0,1:T(8,128)(2,1)}, u32[]{:S(2)}) copy-start(bf16[256,176]{0,1:T(8,128)(2,1)} %get-tuple-element.20) | copy-start | bytes 270340
  214.7 6.5 %copy-start.18 = (bf16[704,64]{0,1:T(8,128)(2,1)S(1)}, bf16[704,64]{0,1:T(8,128)(2,1)}, u32[]{:S(2)}) copy-start(bf16[704,64]{0,1:T(8,128)(2,1)} %get-tuple-element.5) | copy-start | bytes 270340
  221.3 0.9 copy-start.17
  222.2 0.9 copy-start.16
  223.1 0.9 copy-start.15
  223.9 0.9 copy-start.14
  224.8 0.9 copy-start.13
  225.7 0.9 copy-start.12
  226.6 0.9 copy-start.11
Sparse Core Ops, SparseCore 0:
  73.9 94.9 all-reduce.2
